TPU v7x, 32 devices: a whole 2x2x4 slice. The times are simulated.
32 devices in a mesh: req: 8 (over z, y), seq: 4 (over x, core).
Axes of the slice: x: 2, y: 2, z: 4, core: 2. Of those that a mesh axis runs over, the one named last changes fastest.
Arguments:
- queries: bfloat16 [16, 48, 8192], P('req', None, 'seq')
- draft_key_value: bfloat16 [16, 48, 2048], P('req', None, 'seq'), may hold values from -6 to 6
- kv_cache: bfloat16 [16, 8192, 2048], P('req', 'seq')
- cache_lengths: int32 [16], P('req'), may hold values from 2 to 8192, as said below
- ancestors: int32 [16, 48, 48], P('req'), may hold values from 0 to 1, as said below
- dealing: int32 [16], replicated, may hold values from 0 to 15, as said below
- accepted_path: int32 [16, 8], P('req'), may hold values from 0 to 47
Outputs:
- verified_context: bfloat16 [768, 8192], P(('req', 'seq'))
- kept_entries: bfloat16 [16, 8, 2048], P('req', None, 'seq')
Inputs may be any that keep to these rules, and one draw needn't show every extreme that they name: `dealing`: a permutation of the request ids. `cache_lengths`: at least 2 live positions; some slot's cache is full (8192). Each row is the 0/1 indicator of a draft token's ancestors in its tree, the token itself included; token 0 is the root, a token's parent has a lower index.
All inputs are finite; a program needn't handle non-finite values.
Results may differ from a plain program's by a relative error of at most 0.0046.
Values may be sent and summed in bfloat16 or wider, within the bound.
A program may use at most 128 MiB of HBM per device.

v0:
```python
import jax
import jax.numpy as jnp
from jax import lax
from jax.sharding import PartitionSpec as P

HEAD_WIDTH = 128
BLK = 1024


def online_merge(earlier, later):
    max_a, sum_a, acc_a = earlier
    max_b, sum_b, acc_b = later
    row_max = jnp.maximum(max_a, max_b)
    scale_a = jnp.exp(max_a - row_max)
    scale_b = jnp.exp(max_b - row_max)
    return (
        row_max,
        sum_a * scale_a + sum_b * scale_b,
        acc_a * scale_a[..., None] + acc_b * scale_b[..., None],
    )


def block_terms(grouped, key_rows, values, allowed):
    scores = jnp.einsum(
        "tkgd,skd->tkgs", grouped, key_rows, preferred_element_type=jnp.float32
    ) * HEAD_WIDTH ** (-0.5)
    scores = jnp.where(allowed, scores, jnp.float32(-1e30))
    row_max = jnp.max(scores, axis=-1)
    weights = jnp.where(allowed, jnp.exp(scores - row_max[..., None]), jnp.float32(0.0))
    row_sum = jnp.sum(weights, axis=-1)
    row_acc = jnp.einsum(
        "tkgs,skd->tkgd", weights.astype(jnp.bfloat16), values, preferred_element_type=jnp.float32
    )
    return (row_max, row_sum, row_acc)


def attend(query_rows, cache_rows, draft_rows, length, pos_offset, tree_mask, use_draft, blk_size):
    tree_len = query_rows.shape[0]
    kv_heads = cache_rows.shape[1] // (2 * HEAD_WIDTH)
    groups = query_rows.shape[1] // (HEAD_WIDTH * kv_heads)
    grouped = query_rows.reshape(tree_len, kv_heads, groups, HEAD_WIDTH)
    draft_part = draft_rows.reshape(tree_len, kv_heads, 2, HEAD_WIDTH)
    draft_allowed = jnp.logical_and(tree_mask > 0, use_draft)[:, None, None, :]
    running = block_terms(grouped, draft_part[:, :, 0], draft_part[:, :, 1], draft_allowed)
    blk_count = cache_rows.shape[0] // blk_size

    def body_step(blk_index, state):
        blk_start = blk_index * blk_size

        def absorb(state_in):
            cache_piece = lax.dynamic_slice_in_dim(cache_rows, blk_start, blk_size, 0).reshape(
                blk_size, kv_heads, 2, HEAD_WIDTH
            )
            positions = pos_offset + blk_start + jnp.arange(blk_size, dtype=jnp.int32)
            allowed = (positions < length)[None, None, None, :]
            return online_merge(
                state_in, block_terms(grouped, cache_piece[:, :, 0], cache_piece[:, :, 1], allowed)
            )

        return lax.cond(pos_offset + blk_start < length, absorb, lambda state_in: state_in, state)

    return lax.fori_loop(0, blk_count, body_step, running)


def body(queries, draft_key_value, kv_cache, cache_lengths, ancestors, dealing, accepted_path):
    local_reqs = kv_cache.shape[0]
    tree_len = queries.shape[1]
    picker = (
        accepted_path[:, :, None] == jnp.arange(tree_len, dtype=jnp.int32)[None, None, :]
    ).astype(jnp.bfloat16)
    kept_entries = jnp.einsum(
        "rit,rtc->ric", picker, draft_key_value, preferred_element_type=jnp.float32
    ).astype(jnp.bfloat16)
    every_query, every_draft = (
        lax.all_gather(queries, "req", axis=0, tiled=True),
        lax.all_gather(draft_key_value, "req", axis=0, tiled=True),
    )
    chosen = lax.dynamic_slice_in_dim(dealing, lax.axis_index("req") * local_reqs, local_reqs)
    own_query = jnp.stack(
        [
            lax.dynamic_index_in_dim(every_query, chosen[slot], 0, keepdims=False)
            for slot in range(local_reqs)
        ],
        axis=0,
    )
    own_draft = jnp.stack(
        [
            lax.dynamic_index_in_dim(every_draft, chosen[slot], 0, keepdims=False)
            for slot in range(local_reqs)
        ],
        axis=0,
    )
    seq_count = lax.axis_size("seq")
    full_query, full_draft = (
        lax.all_gather(own_query, "seq", axis=2, tiled=True),
        lax.all_gather(own_draft, "seq", axis=2, tiled=True),
    )
    position = lax.axis_index("seq")
    pos_offset = position * kv_cache.shape[1]
    maxima, sums, partials = ([], [], [])
    for slot_index in range(local_reqs):
        row_max, row_sum, row_acc = attend(
            full_query[slot_index],
            kv_cache[slot_index],
            full_draft[slot_index],
            cache_lengths[slot_index],
            pos_offset,
            ancestors[slot_index],
            position == 0,
            BLK,
        )
        maxima.append(row_max.reshape(tree_len, -1))
        sums.append(row_sum.reshape(tree_len, -1))
        partials.append(row_acc.reshape(tree_len, -1))
    all_max = jnp.concatenate(maxima, axis=0)
    all_sum = jnp.concatenate(sums, axis=0)
    all_acc = jnp.concatenate(partials, axis=0)
    head_count = all_max.shape[1]
    recv_acc, recv_max, recv_sum = (
        lax.all_to_all(all_acc[None], "seq", split_axis=1, concat_axis=0, tiled=True),
        lax.all_to_all(all_max[None], "seq", split_axis=1, concat_axis=0, tiled=True),
        lax.all_to_all(all_sum[None], "seq", split_axis=1, concat_axis=0, tiled=True),
    )
    top_max = jnp.max(recv_max, axis=0)
    factors = jnp.exp(recv_max - top_max[None])
    denominator = jnp.sum(factors * recv_sum, axis=0)
    token_count = recv_acc.shape[1]
    numerator = jnp.sum(
        factors[..., None] * recv_acc.reshape(seq_count, token_count, head_count, HEAD_WIDTH),
        axis=0,
    )
    context = (
        (numerator / denominator[..., None])
        .reshape(token_count, head_count * HEAD_WIDTH)
        .astype(jnp.bfloat16)
    )
    return (context, kept_entries)


def solution(mesh):
    placed = (
        P("req", None, "seq"),
        P("req", None, "seq"),
        P("req", "seq", None),
        P("req"),
        P("req", None, None),
        P(),
        P("req", None),
    )
    return jax.shard_map(
        body,
        mesh=mesh,
        in_specs=placed,
        out_specs=(P(("req", "seq"), None), P("req", None, "seq")),
        check_vma=False,
    )
```

profile of v0, /device:TPU:0, one launch (start us, length us, event | category | flops | bytes accessed | tf_op | source)
XLA Modules:
  0.0 253.7 jit_solution(6076901709120950034)
XLA Ops:
  12.8 35.5 %all_gather.12 = bf16[16,48,512]{2,1,0:T(8,128)(2,1)S(1)} all-gather(bf16[2,48,512]{2,1,0:T(8,128)(2,1)} %param.16), channel_id=1, replica_groups=mesh['req'=8,'seq'=4] {'req'}, dimensions={0}, use_global_device_ids=true | all-gather | bytes 884736 | tf_op jit(solution)/shard_map/all_gather | solution.py:76
  48.3 6.3 %all_gather.13 = bf16[2,48,2048]{2,1,0:T(8,128)(2,1)S(1)} all-gather(bf16[2,48,512]{2,1,0:T(8,128)(2,1)S(1)} %pad_maximum_fusion.1), channel_id=1, replica_groups=mesh['req'=8,'seq'=4] {'seq'}, dimensions={2}, use_global_device_ids=true | all-gather | bytes 491520 | tf_op jit(solution)/shard_map/all_gather | solution.py:96
  54.6 24.1 %all-gather.3.cloned.1.call-done = bf16[16,48,2048]{2,1,0:T(8,128)(2,1)} async-done(((bf16[2,48,2048]{2,1,0:T(8,128)(2,1)}), bf16[16,48,2048]{2,1,0:T(8,128)(2,1)}) %all-gather.3.cloned.1.call-update) | async-done | bytes 3145744 | tf_op jit(solution)/shard_map/all_gather | solution.py:75
  80.9 12.1 %fusion.51 = (bf16[1,2048,2048]{2,1,0:T(8,128)(2,1)}, bf16[1,2048,2048]{2,1,0:T(8,128)(2,1)}) fusion(bf16[2,2048,2048]{2,1,0:T(8,128)(2,1)} %param.17), kind=kLoop, calls=%fused_computation.97 | loop fusion | bytes 33554432 | tf_op jit(solution)/shard_map/slice | solution.py:104
  93.0 12.4 %copy.102 = bf16[1,2048,2048]{1,2,0:T(8,128)(2,1)} copy(bf16[1,2048,2048]{2,1,0:T(8,128)(2,1)} %get-tuple-element.463) | data formatting | bytes 16777216
  105.6 12.3 %copy.99 = bf16[1,2048,2048]{1,2,0:T(8,128)(2,1)} copy(bf16[1,2048,2048]{2,1,0:T(8,128)(2,1)} %get-tuple-element.462) | data formatting | bytes 16777216
  124.6 26.6 %while.35 = (s32[]{:T(128)}, f32[48,8,8]{0,2,1:T(8,128)S(1)}, f32[48,8,8]{0,2,1:T(8,128)S(1)}, f32[48,8,8,128]{3,0,2,1:T(8,128)S(1)}, s32[]{:T(128)}, /*index=5*...) while((s32[]{:T(128)}, f32[48,8,8]{0,2,1:T(8,128)S(1)}, ...), condition=%wide.region_15.16_spmd, body=%wide.region_10.15_spmd.sunk | while | flops 1652701184 | bytes 54502720 | solution.py:62
  125.3 12.6 %conditional.5 = ((f32[48,8,8]{0,2,1:T(8,128)S(1)}, f32[48,8,8]{0,2,1:T(8,128)S(1)}, f32[48,8,8,128]{3,0,2,1:T(8,128)S(1)})) conditional(s32[]{:T(128)} %convert_element_type.58, (f32[48,8,8]{0,2,1:T(8,128)S(1)}, f32[48,8,8]{0,2,1:T(8,128)S(1)}, f32[48,8,8,128]{3,0,2,1:T(8,128)S(1)}) %tuple.103, (s32[]{:T(128)}, s32[]{:T(128)}, s32[]{:T(128)}, ...), branch_computations={%region_11.11_spmd, %region_12.14_spmd} | conditional | flops 1652701184 | bytes 54502488 | solution.py:60
  125.9 2.6 %constant_dynamic-slice_fusion.1 = bf16[1024,2048]{0,1:T(8,128)(2,1)S(1)} fusion(bf16[2048,2048]{0,1:T(8,128)(2,1)} %get-tuple-element.338, s32[]{:T(128)S(6)} %select_n.40), kind=kLoop, calls=%fused_computation.42 | loop fusion | bytes 8388612 | tf_op jit(solution)/shard_map/while/body/eval_jaxpr/cond/branch_1_fun/dynamic_slice | solution.py:51
  128.6 2.2 bitcast_reduce_fusion.1
  130.8 3.6 %fusion.18 = f32[48,8,8]{0,2,1:T(8,128)S(1)} fusion(f32[8,1024,48,8]{1,2,3,0:T(8,128)S(1)} %get-tuple-element.461, f32[48,8,8]{0,2,1:T(8,128)S(1)} %get-tuple-element.460, pred[1024]{0:T(1024)(128)(4,1)S(1)} %add_compare_fusion.1), kind=kLoop, calls=%fused_computation.29 | loop fusion | flops 15725568 | bytes 12608512 | tf_op jit(solution)/shard_map/while/body/eval_jaxpr/cond/branch_1_fun/reduce_sum | solution.py:30
  134.5 3.3 %fusion.24 = f32[48,8,8,128]{3,0,2,1:T(8,128)S(1)} fusion(f32[48,8,8,128]{3,0,2,1:T(8,128)S(1)} %get-tuple-element.341, f32[8,1024,48,8]{1,2,3,0:T(8,128)S(1)} %get-tuple-element.461, f32[48,8,8]{0,2,1:T(8,128)S(1)} %get-tuple-element.460, pred[1024]{0:T(1024)(128)(4,1)S(1)} %add_compare_fusion.1, bf16[1024,8,2,128]{0,3,2,1:T(8,128)(2,1)S(1)} %bitcast.163, ...), kind=kOutput, calls=%fused_computation.37 | convolution fusion | flops 822214656 | bytes 17926144 | tf_op jit(solution)/shard_map/while/body/eval_jaxpr/cond/branch_1_fun/tkgs,skd->tkgd/dot_general | solution.py:31
  138.5 12.6 %conditional.5 = ((f32[48,8,8]{0,2,1:T(8,128)S(1)}, f32[48,8,8]{0,2,1:T(8,128)S(1)}, f32[48,8,8,128]{3,0,2,1:T(8,128)S(1)})) conditional(s32[]{:T(128)} %convert_element_type.58, (f32[48,8,8]{0,2,1:T(8,128)S(1)}, f32[48,8,8]{0,2,1:T(8,128)S(1)}, f32[48,8,8,128]{3,0,2,1:T(8,128)S(1)}) %tuple.103, (s32[]{:T(128)}, s32[]{:T(128)}, s32[]{:T(128)}, ...), branch_computations={%region_11.11_spmd, %region_12.14_spmd} | conditional | flops 1652701184 | bytes 54502488 | solution.py:60
  139.2 2.6 %constant_dynamic-slice_fusion.1 = bf16[1024,2048]{0,1:T(8,128)(2,1)S(1)} fusion(bf16[2048,2048]{0,1:T(8,128)(2,1)} %get-tuple-element.338, s32[]{:T(128)S(6)} %select_n.40), kind=kLoop, calls=%fused_computation.42 | loop fusion | bytes 8388612 | tf_op jit(solution)/shard_map/while/body/eval_jaxpr/cond/branch_1_fun/dynamic_slice | solution.py:51
  144.0 3.6 %fusion.18 = f32[48,8,8]{0,2,1:T(8,128)S(1)} fusion(f32[8,1024,48,8]{1,2,3,0:T(8,128)S(1)} %get-tuple-element.461, f32[48,8,8]{0,2,1:T(8,128)S(1)} %get-tuple-element.460, pred[1024]{0:T(1024)(128)(4,1)S(1)} %add_compare_fusion.1), kind=kLoop, calls=%fused_computation.29 | loop fusion | flops 15725568 | bytes 12608512 | tf_op jit(solution)/shard_map/while/body/eval_jaxpr/cond/branch_1_fun/reduce_sum | solution.py:30
  147.7 3.3 %fusion.24 = f32[48,8,8,128]{3,0,2,1:T(8,128)S(1)} fusion(f32[48,8,8,128]{3,0,2,1:T(8,128)S(1)} %get-tuple-element.341, f32[8,1024,48,8]{1,2,3,0:T(8,128)S(1)} %get-tuple-element.461, f32[48,8,8]{0,2,1:T(8,128)S(1)} %get-tuple-element.460, pred[1024]{0:T(1024)(128)(4,1)S(1)} %add_compare_fusion.1, bf16[1024,8,2,128]{0,3,2,1:T(8,128)(2,1)S(1)} %bitcast.163, ...), kind=kOutput, calls=%fused_computation.37 | convolution fusion | flops 822214656 | bytes 17926144 | tf_op jit(solution)/shard_map/while/body/eval_jaxpr/cond/branch_1_fun/tkgs,skd->tkgd/dot_general | solution.py:31
  155.7 26.5 %while.34 = (s32[]{:T(128)}, f32[48,8,8]{0,2,1:T(8,128)S(1)}, f32[48,8,8]{0,2,1:T(8,128)S(1)}, f32[48,8,8,128]{3,0,2,1:T(8,128)S(1)}, s32[]{:T(128)}, /*index=5*...) while((s32[]{:T(128)}, f32[48,8,8]{0,2,1:T(8,128)S(1)}, ...), condition=%wide.region_7.8_spmd, body=%wide.region_2.7_spmd.sunk | while | flops 1652701184 | bytes 54502720 | solution.py:62
  156.4 12.6 %conditional.4 = ((f32[48,8,8]{0,2,1:T(8,128)S(1)}, f32[48,8,8]{0,2,1:T(8,128)S(1)}, f32[48,8,8,128]{3,0,2,1:T(8,128)S(1)})) conditional(s32[]{:T(128)} %convert_element_type.57, (f32[48,8,8]{0,2,1:T(8,128)S(1)}, f32[48,8,8]{0,2,1:T(8,128)S(1)}, f32[48,8,8,128]{3,0,2,1:T(8,128)S(1)}) %tuple.100, (s32[]{:T(128)}, s32[]{:T(128)}, s32[]{:T(128)}, ...), branch_computations={%region_3.3_spmd, %region_4.6_spmd} | conditional | flops 1652701184 | bytes 54502488 | solution.py:60
  157.0 2.6 %constant_dynamic-slice_fusion = bf16[1024,2048]{0,1:T(8,128)(2,1)S(1)} fusion(bf16[2048,2048]{0,1:T(8,128)(2,1)} %get-tuple-element.318, s32[]{:T(128)S(6)} %select_n.36), kind=kLoop, calls=%fused_computation.19 | loop fusion | bytes 8388612 | tf_op jit(solution)/shard_map/while/body/eval_jaxpr/cond/branch_1_fun/dynamic_slice | solution.py:51
  159.7 2.2 bitcast_reduce_fusion
  161.9 3.6 %fusion.3 = f32[48,8,8]{0,2,1:T(8,128)S(1)} fusion(f32[8,1024,48,8]{1,2,3,0:T(8,128)S(1)} %get-tuple-element.459, f32[48,8,8]{0,2,1:T(8,128)S(1)} %get-tuple-element.458, pred[1024]{0:T(1024)(128)(4,1)S(1)} %add_compare_fusion), kind=kLoop, calls=%fused_computation.6 | loop fusion | flops 15725568 | bytes 12608512 | tf_op jit(solution)/shard_map/while/body/eval_jaxpr/cond/branch_1_fun/reduce_sum | solution.py:30
  165.6 3.3 %fusion.9 = f32[48,8,8,128]{3,0,2,1:T(8,128)S(1)} fusion(f32[48,8,8,128]{3,0,2,1:T(8,128)S(1)} %get-tuple-element.321, f32[8,1024,48,8]{1,2,3,0:T(8,128)S(1)} %get-tuple-element.459, f32[48,8,8]{0,2,1:T(8,128)S(1)} %get-tuple-element.458, pred[1024]{0:T(1024)(128)(4,1)S(1)} %add_compare_fusion, bf16[1024,8,2,128]{0,3,2,1:T(8,128)(2,1)S(1)} %bitcast.165, ...), kind=kOutput, calls=%fused_computation.14 | convolution fusion | flops 822214656 | bytes 17926144 | tf_op jit(solution)/shard_map/while/body/eval_jaxpr/cond/branch_1_fun/tkgs,skd->tkgd/dot_general | solution.py:31
  169.6 12.6 %conditional.4 = ((f32[48,8,8]{0,2,1:T(8,128)S(1)}, f32[48,8,8]{0,2,1:T(8,128)S(1)}, f32[48,8,8,128]{3,0,2,1:T(8,128)S(1)})) conditional(s32[]{:T(128)} %convert_element_type.57, (f32[48,8,8]{0,2,1:T(8,128)S(1)}, f32[48,8,8]{0,2,1:T(8,128)S(1)}, f32[48,8,8,128]{3,0,2,1:T(8,128)S(1)}) %tuple.100, (s32[]{:T(128)}, s32[]{:T(128)}, s32[]{:T(128)}, ...), branch_computations={%region_3.3_spmd, %region_4.6_spmd} | conditional | flops 1652701184 | bytes 54502488 | solution.py:60
  170.3 2.6 %constant_dynamic-slice_fusion = bf16[1024,2048]{0,1:T(8,128)(2,1)S(1)} fusion(bf16[2048,2048]{0,1:T(8,128)(2,1)} %get-tuple-element.318, s32[]{:T(128)S(6)} %select_n.36), kind=kLoop, calls=%fused_computation.19 | loop fusion | bytes 8388612 | tf_op jit(solution)/shard_map/while/body/eval_jaxpr/cond/branch_1_fun/dynamic_slice | solution.py:51
  175.1 3.6 %fusion.3 = f32[48,8,8]{0,2,1:T(8,128)S(1)} fusion(f32[8,1024,48,8]{1,2,3,0:T(8,128)S(1)} %get-tuple-element.459, f32[48,8,8]{0,2,1:T(8,128)S(1)} %get-tuple-element.458, pred[1024]{0:T(1024)(128)(4,1)S(1)} %add_compare_fusion), kind=kLoop, calls=%fused_computation.6 | loop fusion | flops 15725568 | bytes 12608512 | tf_op jit(solution)/shard_map/while/body/eval_jaxpr/cond/branch_1_fun/reduce_sum | solution.py:30
  178.8 3.3 %fusion.9 = f32[48,8,8,128]{3,0,2,1:T(8,128)S(1)} fusion(f32[48,8,8,128]{3,0,2,1:T(8,128)S(1)} %get-tuple-element.321, f32[8,1024,48,8]{1,2,3,0:T(8,128)S(1)} %get-tuple-element.459, f32[48,8,8]{0,2,1:T(8,128)S(1)} %get-tuple-element.458, pred[1024]{0:T(1024)(128)(4,1)S(1)} %add_compare_fusion, bf16[1024,8,2,128]{0,3,2,1:T(8,128)(2,1)S(1)} %bitcast.165, ...), kind=kOutput, calls=%fused_computation.14 | convolution fusion | flops 822214656 | bytes 17926144 | tf_op jit(solution)/shard_map/while/body/eval_jaxpr/cond/branch_1_fun/tkgs,skd->tkgd/dot_general | solution.py:31
  186.1 3.5 %all-to-all-start.2 = ((f32[4,1,1536]{2,1,0:T(1,128)}), f32[4,1,1536]{2,1,0:T(1,128)S(1)}, u32[]{:S(2)}, u32[]{:S(2)}) async-start(f32[4,1,1536]{2,1,0:T(1,128)} %reshape.123), calls=%async_computation.2 | async-start | bytes 49152 | tf_op jit(solution)/shard_map/all_to_all | solution.py:122
  189.6 4.1 %copy_bitcast_fusion = (f32[48,8192]{1,0:T(8,128)S(1)}, f32[48,8192]{1,0:T(8,128)S(1)}) fusion(f32[6,8,64,128]{3,2,1,0:T(8,128)} %bitcast.173, f32[6,8,64,128]{3,2,1,0:T(8,128)} %bitcast.174), kind=kLoop, calls=%fused_computation.48 | loop fusion | bytes 6291456 | tf_op jit(solution)/shard_map/reshape | solution.py:114
  195.3 3.3 %all-to-all-start = ((f32[4,1,1536]{2,1,0:T(1,128)}), f32[4,1,1536]{2,1,0:T(1,128)S(1)}, u32[]{:S(2)}, u32[]{:S(2)}) async-start(f32[4,1,1536]{2,1,0:T(1,128)} %reshape.121), calls=%async_computation | async-start | bytes 49152 | tf_op jit(solution)/shard_map/all_to_all | solution.py:121
  198.8 4.9 %copy.81 = f32[1,96,8192]{2,0,1:T(1,128)} copy(f32[1,96,8192]{2,1,0:T(8,128)S(1)} %maximum_bitcast_fusion) | data formatting | bytes 6291456 | tf_op jit(solution)/shard_map/broadcast_in_dim | solution.py:120
  203.8 3.8 %all-to-all-start.1 = ((f32[1,96,8192]{2,0,1:T(1,128)}), f32[1,96,8192]{2,0,1:T(1,128)S(1)}, u32[]{:S(2)}, u32[]{:S(2)}) async-start(f32[1,96,8192]{2,0,1:T(1,128)} %copy.81), calls=%async_computation.1 | async-start | bytes 6291456 | tf_op jit(solution)/shard_map/all_to_all | solution.py:120
  210.2 34.3 %all-to-all-done.1 = f32[1,96,8192]{2,0,1:T(1,128)S(1)} async-done(((f32[1,96,8192]{2,0,1:T(1,128)}), f32[1,96,8192]{2,0,1:T(1,128)S(1)}, u32[]{:S(2)}, u32[]{:S(2)}) %all-to-all-start.1) | async-done | bytes 3145760 | tf_op jit(solution)/shard_map/all_to_all | solution.py:120
  (77 shorter events, 33.2 us)
Async XLA Ops:
  7.2 73.6 %copy-start.3 = (s32[2,48,48]{2,1,0:T(8,128)S(1)}, s32[2,48,48]{2,1,0:T(8,128)}, u32[]{:S(2)}) copy-start(s32[2,48,48]{2,1,0:T(8,128)} %param.19) | copy-start | bytes 55300
  7.2 71.5 %all-gather.3.cloned.1.call-start = ((), (), s32[]{:S(2)}) async-start(), calls=%async_computation.3 | async-start | bytes 3538944 | tf_op jit(solution)/shard_map/all_gather | solution.py:75
  7.9 112.5 %all-gather.5.cloned.1.call-start = ((), (), s32[]{:S(2)}) async-start(), calls=%async_computation.4 | async-start | bytes 1966080 | tf_op jit(solution)/shard_map/all_gather | solution.py:95
  105.6 12.3 %copy-start.4 = (s32[2]{0:T(128)S(1)}, s32[2]{0:T(128)}, u32[]{:S(2)}) copy-start(s32[2]{0:T(128)} %param.18) | copy-start | bytes 28
  122.1 2.0 copy-start.1
  151.3 2.4 copy-start
  186.1 9.2 %all-to-all-start.2 = ((f32[4,1,1536]{2,1,0:T(1,128)}), f32[4,1,1536]{2,1,0:T(1,128)S(1)}, u32[]{:S(2)}, u32[]{:S(2)}) async-start(f32[4,1,1536]{2,1,0:T(1,128)} %reshape.123), calls=%async_computation.2 | async-start | bytes 49152 | tf_op jit(solution)/shard_map/all_to_all | solution.py:122
  195.3 8.4 %all-to-all-start = ((f32[4,1,1536]{2,1,0:T(1,128)}), f32[4,1,1536]{2,1,0:T(1,128)S(1)}, u32[]{:S(2)}, u32[]{:S(2)}) async-start(f32[4,1,1536]{2,1,0:T(1,128)} %reshape.121), calls=%async_computation | async-start | bytes 49152 | tf_op jit(solution)/shard_map/all_to_all | solution.py:121
  203.8 3.8 %copy-start.2 = (bf16[2,48,512]{2,1,0:T(8,128)(2,1)S(1)}, bf16[2,48,512]{2,1,0:T(8,128)(2,1)}, u32[]{:S(2)}) copy-start(bf16[2,48,512]{2,1,0:T(8,128)(2,1)} %param.16) | copy-start | bytes 294916
  203.8 3.9 %copy-start.5 = (s32[2,8]{1,0:T(2,128)S(1)}, s32[2,8]{1,0:T(2,128)}, u32[]{:S(2)}) copy-start(s32[2,8]{1,0:T(2,128)} %param.21) | copy-start | bytes 196
  203.8 40.7 %all-to-all-start.1 = ((f32[1,96,8192]{2,0,1:T(1,128)}), f32[1,96,8192]{2,0,1:T(1,128)S(1)}, u32[]{:S(2)}, u32[]{:S(2)}) async-start(f32[1,96,8192]{2,0,1:T(1,128)} %copy.81), calls=%async_computation.1 | async-start | bytes 6291456 | tf_op jit(solution)/shard_map/all_to_all | solution.py:120
Sparse Core Ops, SparseCore 0:
  10.2 68.4 all-gather.2
  80.9 18.2 all-gather.4
where the time goes:
time: 255 us; the launch traced here: 254 us
  local copies, waits for them, and re-layouts  71.2 us (28%)
  waiting for transfers between devices  59.1 us (23%)
  blocking collectives  41.8 us (16%)
  matrix products  26.1 us (10%)
  other arithmetic  23.8 us (9%)
  between operations  18 us (7%)
  starting transfers between devices  10.6 us (4%)
  loops' own time  3.06 us (1%)
    all_gather x1, blocking collectives, body(): lax.all_gather(draft_key_value, 'req', axis=0, tiled=True)  35.5 us
    all_to_all x1, waiting for transfers between devices, body(): lax.all_to_all(all_acc[None], 'seq', split_axis=1, concat_axis=0, tiled=T...  34.3 us
    unnamed x23, local copies, waits for them, and re-layouts  29.7 us
    all_gather x1, waiting for transfers between devices, body(): lax.all_gather(queries, 'req', axis=0, tiled=True)  24.1 us
    reduce_sum x6, other arithmetic, block_terms(): row_sum = jnp.sum(weights, axis=-1)  15.4 us
    dot_general x6, matrix products, block_terms(): jnp.einsum('tkgs,skd->tkgd', weights.astype(jnp.bfloat16), values, prefer...  14.4 us
    slice x1, local copies, waits for them, and re-layouts, body(): kv_cache[slot_index]  12.1 us
    dot_general x6, matrix products, block_terms(): jnp.einsum('tkgd,skd->tkgs', grouped, key_rows, preferred_element_type=jn...  11 us
  transfers between devices with their start and end apart: 5, of which 2 were waited for; matrix products, arithmetic and copies ran while one was open for 21% of the time, Pallas kernels for 0%

commit v1 on v0

--- a/solution.py
+++ b/solution.py
@@ -1,6 +1,11 @@
+import functools
+import math
+
 import jax
 import jax.numpy as jnp
 from jax import lax
+from jax.experimental import pallas as pl
+from jax.experimental.pallas import tpu as pltpu
 from jax.sharding import PartitionSpec as P
 
 HEAD_WIDTH = 128
@@ -62,7 +67,7 @@
     return lax.fori_loop(0, blk_count, body_step, running)
 
 
-def body(queries, draft_key_value, kv_cache, cache_lengths, ancestors, dealing, accepted_path):
+def plain_body(queries, draft_key_value, kv_cache, cache_lengths, ancestors, dealing, accepted_path):
     local_reqs = kv_cache.shape[0]
     tree_len = queries.shape[1]
     picker = (
@@ -137,6 +142,330 @@
     return (context, kept_entries)
 
 
+MESH = pl.DeviceIdType.MESH
+TOK = 48
+HALF = TOK // 2
+ROWS = 8 * HALF
+NEG = -1e30
+SCALE2 = HEAD_WIDTH ** (-0.5) * math.log2(math.e)
+GROUPS = 8
+QUARTERS = 4
+ROW_CHUNKS = 2
+
+
+def fused_kernel(
+    deal, lens, q_ref, d_ref, kv_ref, anc_ref, out_ref,
+    r1q, r1d, s2q, s2d, qf, df, kvb, accs, rbuf, stats, rstat,
+    s1, r1, s1d, r1ds, s2, r2, s2ds, r2ds, cs, cr, xs, xr, fs, fr, kvs,
+    os0, os1, os2, ors, ss, srs,
+):
+    g = lax.axis_index("req")
+    q = lax.axis_index("seq")
+    xx, cc = q // 2, q % 2
+    core = xx * 2 + (1 - cc)
+    xpart = (1 - xx) * 2 + cc
+    xcore = (1 - xx) * 2 + (1 - cc)
+
+    barrier = pltpu.get_barrier_semaphore()
+    for o in range(1, GROUPS):
+        pl.semaphore_signal(barrier, inc=1, device_id=(lax.rem(g + o, GROUPS), q), device_id_type=MESH)
+    for other in (core, xpart, xcore):
+        pl.semaphore_signal(barrier, inc=1, device_id=(g, other), device_id_type=MESH)
+    pl.semaphore_wait(barrier, GROUPS + 2)
+
+    def relays(i):
+        return i % 2 == (i // 2) % 2
+
+    def remote(src, dst, send, recv, dev):
+        return pltpu.make_async_remote_copy(
+            src_ref=src, dst_ref=dst, send_sem=send, recv_sem=recv, device_id=dev, device_id_type=MESH
+        )
+
+    def first_q(o):
+        i = lax.rem(g + o, GROUPS)
+        return remote(
+            q_ref.at[:, :, pl.ds(pl.multiple_of(i * 256, 256), 256)], r1q.at[pl.ds(2 * g, 2)],
+            s1.at[o], r1.at[o], (i, q),
+        )
+
+    def first_d(o):
+        i = lax.rem(g + o, GROUPS)
+        return remote(
+            d_ref.at[:, :, pl.ds(pl.multiple_of((i // 2) * 128, 128), 128)], r1d.at[pl.ds(2 * g, 2)],
+            s1d.at[o], r1ds.at[o], (i, q),
+        )
+
+    def kv_copy(slot, k):
+        return pltpu.make_async_copy(
+            kv_ref.at[slot, :, pl.ds(pl.multiple_of(k * 256, 256), 256)],
+            kvb.at[slot * 8 + k], kvs.at[slot * 8 + k],
+        )
+
+    for o in range(1, GROUPS):
+        first_q(o).start()
+
+        @pl.when(relays(lax.rem(g + o, GROUPS)))
+        def _():
+            first_d(o).start()
+
+    def start_kv(n, carry):
+        kv_copy(n // 8, n % 8).start()
+        return carry
+
+    lax.fori_loop(0, 16, start_kv, 0)
+    r1q[pl.ds(2 * g, 2)] = q_ref[:, :, pl.ds(pl.multiple_of(g * 256, 256), 256)]
+    r1d[pl.ds(2 * g, 2)] = d_ref[:, :, pl.ds(pl.multiple_of((g // 2) * 128, 128), 128)]
+    for part in range(2):
+        for half in range(2):
+            stats[part, half] = jnp.ones_like(stats[part, half])
+
+    for o in range(1, GROUPS):
+        first_q(o).wait_recv()
+
+        @pl.when(relays(g))
+        def _():
+            first_d(o).wait_recv()
+
+    def second_q(o):
+        d = lax.rem(g + o, GROUPS)
+        return remote(
+            s2q.at[d], qf.at[:, pl.ds(q * 16 + g * 2, 2)], s2.at[o], r2.at[o], (d, q)
+        )
+
+    def second_d(o):
+        d = lax.rem(g + o, GROUPS)
+        return remote(s2d.at[d], df.at[:, g // 2], s2ds.at[o], r2ds.at[o], (d, q))
+
+    for o in list(range(1, GROUPS)) + [0]:
+        d = lax.rem(g + o, GROUPS)
+        for j in range(2):
+            r = deal[2 * d + j]
+            piece = r1q[r]
+            if o == 0:
+                qf[j, q * 16 + g * 2] = piece[:, :128]
+                qf[j, q * 16 + g * 2 + 1] = piece[:, 128:]
+            else:
+                s2q[d, j, 0] = piece[:, :128]
+                s2q[d, j, 1] = piece[:, 128:]
+        if o:
+            second_q(o).start()
+
+        @pl.when(relays(g))
+        def _():
+            for j in range(2):
+                r = deal[2 * d + j]
+                if o == 0:
+                    df[j, g // 2] = r1d[r]
+                else:
+                    s2d[d, j] = r1d[r]
+            if o:
+                second_d(o).start()
+
+    def spread(o, owner, send, recv, to):
+        src = lax.rem(g + GROUPS - o, GROUPS)
+        part = qf.at[:, pl.ds(owner * 16 + src * 2, 2)]
+        return remote(part, part, send.at[o], recv.at[o], (g, to))
+
+    for o in range(GROUPS):
+        if o:
+            second_q(o).wait_recv()
+        spread(o, q, xs, xr, xpart).start()
+        spread(o, q, cs, cr, core).start()
+    for o in range(1, GROUPS):
+
+        @pl.when(relays(lax.rem(g + GROUPS - o, GROUPS)))
+        def _():
+            second_d(o).wait_recv()
+
+    def acc_send(slot, half, k, sem, to):
+        return remote(accs.at[slot, half, k], rbuf.at[q, k], sem.at[k], ors.at[q, k], (g, to))
+
+    def step(slot, k, own):
+        kv_copy(slot, k).wait()
+        keys = kvb[slot * 8 + k, :, :128]
+        values = jnp.concatenate(
+            [kvb[slot * 8 + k, :, 128:], jnp.ones((2048, 128), jnp.bfloat16)], axis=1
+        )
+        where_pos = lax.broadcasted_iota(jnp.int32, (1, 2048), 1) + q * 2048
+        bias = jnp.where(where_pos < lens[slot], jnp.float32(0.0), jnp.float32(NEG))
+        tree = jnp.where(
+            jnp.logical_and(anc_ref[slot] > 0, jnp.full((TOK, TOK), own, jnp.int32) > 0),
+            jnp.float32(0.0), jnp.float32(NEG),
+        )
+        dk = df[slot, (k % 2) * 2]
+        dv = jnp.concatenate([df[slot, (k % 2) * 2 + 1], jnp.ones((TOK, 128), jnp.bfloat16)], axis=1)
+        lane = lax.broadcasted_iota(jnp.int32, (HALF, 128), 1)
+        heads = 8 // ROW_CHUNKS
+        rows = heads * TOK
+        contract = (((1,), (1,)), ((), ()))
+        for part in range(ROW_CHUNKS):
+            qs = qf[slot, pl.ds(k * 8 + part * heads, heads)].reshape(rows, 128)
+            s = lax.dot_general(qs, keys, contract, preferred_element_type=jnp.float32) + bias
+            t = lax.dot_general(qs, dk, contract, preferred_element_type=jnp.float32)
+            t = (t.reshape(heads, TOK, TOK) + tree[None]).reshape(rows, TOK)
+            m = jnp.maximum(jnp.max(s, axis=1, keepdims=True), jnp.max(t, axis=1, keepdims=True))
+            p = jnp.exp2((s - m) * SCALE2).astype(jnp.bfloat16)
+            pt = jnp.exp2((t - m) * SCALE2).astype(jnp.bfloat16)
+            o = lax.dot_general(p, values, (((1,), (0,)), ((), ())), preferred_element_type=jnp.float32)
+            o = o + lax.dot_general(pt, dv, (((1,), (0,)), ((), ())), preferred_element_type=jnp.float32)
+            o3 = o.reshape(heads, TOK, 256)
+            m3 = jnp.broadcast_to(m, (rows, 128)).reshape(heads, TOK, 128)
+            for half in range(2):
+                cut = slice(half * HALF, (half + 1) * HALF)
+                accs[slot, half, k, pl.ds(part * heads * HALF, heads * HALF)] = (
+                    o3[:, cut, :128].reshape(heads * HALF, 128).astype(jnp.bfloat16)
+                )
+                ms, ls = stats[slot, half, 0], stats[slot, half, 1]
+                for hh in range(heads):
+                    here = lane == k * 8 + part * heads + hh
+                    ms = jnp.where(here, m3[hh, cut], ms)
+                    ls = jnp.where(here, o3[hh, cut, 128:], ls)
+                stats[slot, half, 0] = ms
+                stats[slot, half, 1] = ls
+
+    def quarter(t, carry):
+        @pl.when(t == 1)
+        def _():
+            for o in range(GROUPS):
+                spread(o, xpart, xs, xr, q).wait_recv()
+                spread(o, xpart, fs, fr, core).start()
+            for o in range(GROUPS):
+                spread(o, core, cs, cr, q).wait_recv()
+
+        @pl.when(t == 3)
+        def _():
+            for o in range(GROUPS):
+                spread(o, xcore, fs, fr, q).wait_recv()
+
+        holder = ((xx + t // 2) % 2) * 2 + (cc + t) % 2
+        own = jnp.where(t == 0, 1, 0).astype(jnp.int32)
+
+        def one(n, inner):
+            k = holder * 2 + n % 2
+            slot = (xx + 1 + n // 2) % 2
+            step(slot, k, own)
+
+            @pl.when(n < 2)
+            def _():
+                acc_send(slot, 0, k, os0, (1 - xx) * 2).start()
+                acc_send(slot, 1, k, os1, (1 - xx) * 2 + 1).start()
+
+            @pl.when(n >= 2)
+            def _():
+                acc_send(slot, 1 - cc, k, os2, core).start()
+
+            return inner
+
+        return lax.fori_loop(0, 4, one, carry)
+
+    lax.fori_loop(0, 4, quarter, 0)
+
+    def stat_send(slot, half, n, to):
+        return remote(stats.at[slot, half], rstat.at[q], ss.at[n], srs.at[q], (g, to))
+
+    stat_send(1 - xx, 0, 0, (1 - xx) * 2).start()
+    stat_send(1 - xx, 1, 1, (1 - xx) * 2 + 1).start()
+    stat_send(xx, 1 - cc, 2, core).start()
+
+    def from_stat(other):
+        return remote(stats.at[0, 0], rstat.at[other], ss.at[0], srs.at[other], (g, q))
+
+    for other in (core, xpart, xcore):
+        from_stat(other).wait_recv()
+    tops = [stats[xx, cc, 0]] + [rstat[other, 0] for other in (core, xpart, xcore)]
+    sums = [stats[xx, cc, 1]] + [rstat[other, 1] for other in (core, xpart, xcore)]
+    top = functools.reduce(jnp.maximum, tops)
+    factors = [jnp.exp2((m - top) * SCALE2) for m in tops]
+    total = sum(f * l for f, l in zip(factors, sums))
+    factors = [f / total for f in factors]
+
+    for k in range(8):
+        for other in (core, xpart, xcore):
+            remote(accs.at[0, 0, k], rbuf.at[other, k], os0.at[k], ors.at[other, k], (g, q)).wait_recv()
+        terms = [accs[xx, cc, k]] + [rbuf[other, k] for other in (core, xpart, xcore)]
+        terms = [term.astype(jnp.float32).reshape(8, HALF, 128) for term in terms]
+        for hh in range(8):
+            h = k * 8 + hh
+            value = sum(f[:, h : h + 1] * term[hh] for f, term in zip(factors, terms))
+            out_ref[:, h * 128 : (h + 1) * 128] = value.astype(jnp.bfloat16)
+
+    for o in range(1, GROUPS):
+        first_q(o).wait_send()
+        second_q(o).wait_send()
+
+        @pl.when(relays(lax.rem(g + o, GROUPS)))
+        def _():
+            first_d(o).wait_send()
+
+        @pl.when(relays(g))
+        def _():
+            second_d(o).wait_send()
+
+    for o in range(GROUPS):
+        spread(o, q, xs, xr, xpart).wait_send()
+        spread(o, q, cs, cr, core).wait_send()
+        spread(o, xpart, fs, fr, core).wait_send()
+    for k in range(8):
+        acc_send(1 - xx, 0, k, os0, (1 - xx) * 2).wait_send()
+        acc_send(1 - xx, 1, k, os1, (1 - xx) * 2 + 1).wait_send()
+        acc_send(xx, 1 - cc, k, os2, core).wait_send()
+    stat_send(1 - xx, 0, 0, (1 - xx) * 2).wait_send()
+    stat_send(1 - xx, 1, 1, (1 - xx) * 2 + 1).wait_send()
+    stat_send(xx, 1 - cc, 2, core).wait_send()
+
+
+def fused(queries, draft_key_value, kv_cache, cache_lengths, ancestors, dealing):
+    dma = pltpu.SemaphoreType.DMA
+    bf = jnp.bfloat16
+    vm = pl.BlockSpec(memory_space=pltpu.VMEM)
+    sm = pl.BlockSpec(memory_space=pltpu.SMEM)
+    return pl.pallas_call(
+        fused_kernel,
+        out_shape=jax.ShapeDtypeStruct((HALF, 8192), bf),
+        in_specs=[sm, sm, vm, vm, pl.BlockSpec(memory_space=pl.ANY), vm],
+        out_specs=vm,
+        scratch_shapes=[
+            pltpu.VMEM((16, TOK, 256), bf),
+            pltpu.VMEM((16, TOK, 128), bf),
+            pltpu.VMEM((GROUPS, 2, 2, TOK, 128), bf),
+            pltpu.VMEM((GROUPS, 2, TOK, 128), bf),
+            pltpu.VMEM((2, 64, TOK, 128), bf),
+            pltpu.VMEM((2, 4, TOK, 128), bf),
+            pltpu.VMEM((16, 2048, 256), bf),
+            pltpu.VMEM((2, 2, 8, ROWS, 128), bf),
+            pltpu.VMEM((QUARTERS, 8, ROWS, 128), bf),
+            pltpu.VMEM((2, 2, 2, HALF, 128), jnp.float32),
+            pltpu.VMEM((QUARTERS, 2, HALF, 128), jnp.float32),
+        ]
+        + [dma((GROUPS,))] * 14
+        + [dma((16,)), dma((8,)), dma((8,)), dma((8,)), dma((QUARTERS, 8)), dma((3,)), dma((QUARTERS,))],
+        compiler_params=pltpu.CompilerParams(
+            collective_id=0, has_side_effects=True, vmem_limit_bytes=56 * 1024 * 1024
+        ),
+        cost_estimate=pl.CostEstimate(flops=2 * 10**9, bytes_accessed=18 * 10**6, transcendentals=13 * 10**6),
+    )(dealing, cache_lengths, queries, draft_key_value, kv_cache, ancestors)
+
+
+def body(groups, quarters, queries, draft_key_value, kv_cache, cache_lengths, ancestors, dealing, accepted_path):
+    args = (queries, draft_key_value, kv_cache, cache_lengths, ancestors, dealing, accepted_path)
+    fits = (
+        groups == GROUPS
+        and quarters == QUARTERS
+        and queries.shape == (2, TOK, 2048)
+        and kv_cache.shape == (2, 2048, 2048)
+    )
+    if not fits:
+        return plain_body(*args)
+    picker = (
+        accepted_path[:, :, None] == jnp.arange(TOK, dtype=jnp.int32)[None, None, :]
+    ).astype(jnp.bfloat16)
+    kept_entries = jnp.einsum(
+        "rit,rtc->ric", picker, draft_key_value, preferred_element_type=jnp.float32
+    ).astype(jnp.bfloat16)
+    context = fused(queries, draft_key_value, kv_cache, cache_lengths, ancestors, dealing)
+    return (context, kept_entries)
+
+
 def solution(mesh):
     placed = (
         P("req", None, "seq"),
@@ -148,7 +477,7 @@
         P("req", None),
     )
     return jax.shard_map(
-        body,
+        functools.partial(body, mesh.shape["req"], mesh.shape["seq"]),
         mesh=mesh,
         in_specs=placed,
         out_specs=(P(("req", "seq"), None), P("req", None, "seq")),

time: 255 us -> 67.6 us (0.27)
  the two profiles are of different devices: /device:TPU:0 before, /device:TPU:29 now
where the time goes in v1:
time: 67.6 us; the launch traced here: 67.4 us
  Pallas kernels  64.2 us (95%)
  local copies, waits for them, and re-layouts  1.77 us (3%)
  matrix products  0.8 us (1%)
    pallas_call x1, Pallas kernels, fused(): pl.pallas_call(fused_kernel, out_shape=jax.ShapeDtypeStruct((HALF, 8192),...  64.2 us
    unnamed x5, local copies, waits for them, and re-layouts  1.77 us

profile of v1, /device:TPU:29, one launch (start us, length us, event | category | flops | bytes accessed | tf_op | source)
XLA Modules:
  0.0 67.4 jit_solution(16004566267839675245)
XLA Ops:
  0.6 0.0 copy-start
  0.6 0.0 copy-start.1
  0.7 64.2 %shard_map.86 = bf16[24,8192]{1,0:T(8,128)(2,1)} custom-call(s32[16]{0:T(128)} %deal.1, s32[2]{0:T(128)} %lens.1, bf16[2,48,2048]{2,1,0:T(8,128)(2,1)} %q_ref.1, bf16[2,48,512]{2,1,0:T(8,128)(2,1)} %d_ref.1, bf16[2,2048,2048]{2,1,0:T(8,128)(2,1)} %kv_ref.1, s32[2,48,48]{2,1,0:T(8,128)} %anc_ref.1), custom_call_target="tpu_custom_call" | custom-call | flops 2000000000 | bytes 18000000 | tf_op jit(solution)/shard_map/pallas_call | solution.py:422
  64.9 0.0 copy-done
  64.9 0.0 copy-done.1
  64.9 0.8 %convolution_convert_fusion = bf16[2,8,512]{2,1,0:T(8,128)(2,1)} fusion(bf16[2,48,512]{2,1,0:T(8,128)(2,1)S(1)} %copy-done, s32[2,8]{1,0:T(2,128)S(1)} %copy-done.1), kind=kOutput, calls=%fused_computation | convolution fusion | flops 795392 | bytes 114752 | tf_op jit(solution)/shard_map/rit,rtc->ric/dot_general | solution.py:462
  65.7 1.8 %copy.10 = bf16[24,8192]{1,0:T(8,128)(2,1)} copy(bf16[24,8192]{1,0:T(8,128)(2,1)} %shard_map.86) | data formatting | bytes 786432
Async XLA Ops:
  0.6 64.2 %copy-start = (bf16[2,48,512]{2,1,0:T(8,128)(2,1)S(1)}, bf16[2,48,512]{2,1,0:T(8,128)(2,1)}, u32[]{:S(2)}) copy-start(bf16[2,48,512]{2,1,0:T(8,128)(2,1)} %d_ref.1) | copy-start | bytes 294916
  0.6 64.2 %copy-start.1 = (s32[2,8]{1,0:T(2,128)S(1)}, s32[2,8]{1,0:T(2,128)}, u32[]{:S(2)}) copy-start(s32[2,8]{1,0:T(2,128)} %param.13) | copy-start | bytes 196

commit v2 on v1

--- a/solution.py
+++ b/solution.py
@@ -156,7 +156,7 @@
 def fused_kernel(
     deal, lens, q_ref, d_ref, kv_ref, anc_ref, out_ref,
     r1q, r1d, s2q, s2d, qf, df, kvb, accs, rbuf, stats, rstat,
-    s1, r1, s1d, r1ds, s2, r2, s2ds, r2ds, cs, cr, xs, xr, fs, fr, kvs,
+    s1, r1, s1d, r1ds, s2, r2, s2ds, r2ds, xs, xr, kvs, ks, kr,
     os0, os1, os2, ors, ss, srs,
 ):
     g = lax.axis_index("req")
@@ -195,10 +195,25 @@
             s1d.at[o], r1ds.at[o], (i, q),
         )
 
-    def kv_copy(slot, k):
+    def columns(parity, kl):
+        k = 2 * parity + 4 * (kl // 2) + kl % 2
+        return pl.ds(pl.multiple_of(k * 256, 256), 256)
+
+    def kv_copy(slot, kl):
         return pltpu.make_async_copy(
-            kv_ref.at[slot, :, pl.ds(pl.multiple_of(k * 256, 256), 256)],
-            kvb.at[slot * 8 + k], kvs.at[slot * 8 + k],
+            kv_ref.at[slot, :, columns(cc, kl)], kvb.at[slot * 4 + kl, cc], kvs.at[slot * 4 + kl]
+        )
+
+    def kv_swap(slot, kl):
+        n = slot * 4 + kl
+        return remote(
+            kv_ref.at[slot, :, columns(1 - cc, kl)], kvb.at[n, cc], ks.at[n], kr.at[n], (g, core)
+        )
+
+    def kv_arrival(slot, kl):
+        n = slot * 4 + kl
+        return remote(
+            kv_ref.at[slot, :, columns(cc, kl)], kvb.at[n, 1 - cc], ks.at[n], kr.at[n], (g, core)
         )
 
     for o in range(1, GROUPS):
@@ -209,10 +224,11 @@
             first_d(o).start()
 
     def start_kv(n, carry):
-        kv_copy(n // 8, n % 8).start()
+        kv_swap(n // 4, n % 4).start()
+        kv_copy(n // 4, n % 4).start()
         return carry
 
-    lax.fori_loop(0, 16, start_kv, 0)
+    lax.fori_loop(0, 8, start_kv, 0)
     r1q[pl.ds(2 * g, 2)] = q_ref[:, :, pl.ds(pl.multiple_of(g * 256, 256), 256)]
     r1d[pl.ds(2 * g, 2)] = d_ref[:, :, pl.ds(pl.multiple_of((g // 2) * 128, 128), 128)]
     for part in range(2):
@@ -270,24 +286,20 @@
         if o:
             second_q(o).wait_recv()
         spread(o, q, xs, xr, xpart).start()
-        spread(o, q, cs, cr, core).start()
     for o in range(1, GROUPS):
 
         @pl.when(relays(lax.rem(g + GROUPS - o, GROUPS)))
         def _():
             second_d(o).wait_recv()
 
-    def acc_send(slot, half, k, sem, to):
-        return remote(accs.at[slot, half, k], rbuf.at[q, k], sem.at[k], ors.at[q, k], (g, to))
-
-    def step(slot, k, own):
-        kv_copy(slot, k).wait()
-        keys = kvb[slot * 8 + k, :, :128]
-        values = jnp.concatenate(
-            [kvb[slot * 8 + k, :, 128:], jnp.ones((2048, 128), jnp.bfloat16)], axis=1
-        )
-        where_pos = lax.broadcasted_iota(jnp.int32, (1, 2048), 1) + q * 2048
-        bias = jnp.where(where_pos < lens[slot], jnp.float32(0.0), jnp.float32(NEG))
+    def acc_send(slot, half, kl, sem, to):
+        return remote(accs.at[slot, half, kl], rbuf.at[q, kl], sem.at[kl], ors.at[q, kl], (g, to))
+
+    def step(slot, k, kl, own):
+        kv_copy(slot, kl).wait()
+        kv_arrival(slot, kl).wait_recv()
+        ones = jnp.ones((2048, 128), jnp.bfloat16)
+        where_pos = lax.broadcasted_iota(jnp.int32, (1, 2048), 1) + xx * 4096
         tree = jnp.where(
             jnp.logical_and(anc_ref[slot] > 0, jnp.full((TOK, TOK), own, jnp.int32) > 0),
             jnp.float32(0.0), jnp.float32(NEG),
@@ -298,21 +310,30 @@
         heads = 8 // ROW_CHUNKS
         rows = heads * TOK
         contract = (((1,), (1,)), ((), ()))
+        plain = (((1,), (0,)), ((), ()))
         for part in range(ROW_CHUNKS):
             qs = qf[slot, pl.ds(k * 8 + part * heads, heads)].reshape(rows, 128)
-            s = lax.dot_general(qs, keys, contract, preferred_element_type=jnp.float32) + bias
             t = lax.dot_general(qs, dk, contract, preferred_element_type=jnp.float32)
             t = (t.reshape(heads, TOK, TOK) + tree[None]).reshape(rows, TOK)
-            m = jnp.maximum(jnp.max(s, axis=1, keepdims=True), jnp.max(t, axis=1, keepdims=True))
-            p = jnp.exp2((s - m) * SCALE2).astype(jnp.bfloat16)
+            m = jnp.max(t, axis=1, keepdims=True)
+            scores = []
+            for b in range(2):
+                s = lax.dot_general(
+                    qs, kvb[slot * 4 + kl, b, :, :128], contract, preferred_element_type=jnp.float32
+                ) + jnp.where(where_pos + b * 2048 < lens[slot], jnp.float32(0.0), jnp.float32(NEG))
+                m = jnp.maximum(m, jnp.max(s, axis=1, keepdims=True))
+                scores.append(s)
             pt = jnp.exp2((t - m) * SCALE2).astype(jnp.bfloat16)
-            o = lax.dot_general(p, values, (((1,), (0,)), ((), ())), preferred_element_type=jnp.float32)
-            o = o + lax.dot_general(pt, dv, (((1,), (0,)), ((), ())), preferred_element_type=jnp.float32)
+            o = lax.dot_general(pt, dv, plain, preferred_element_type=jnp.float32)
+            for b in range(2):
+                p = jnp.exp2((scores[b] - m) * SCALE2).astype(jnp.bfloat16)
+                values = jnp.concatenate([kvb[slot * 4 + kl, b, :, 128:], ones], axis=1)
+                o = o + lax.dot_general(p, values, plain, preferred_element_type=jnp.float32)
             o3 = o.reshape(heads, TOK, 256)
             m3 = jnp.broadcast_to(m, (rows, 128)).reshape(heads, TOK, 128)
             for half in range(2):
                 cut = slice(half * HALF, (half + 1) * HALF)
-                accs[slot, half, k, pl.ds(part * heads * HALF, heads * HALF)] = (
+                accs[slot, half, kl, pl.ds(part * heads * HALF, heads * HALF)] = (
                     o3[:, cut, :128].reshape(heads * HALF, 128).astype(jnp.bfloat16)
                 )
                 ms, ls = stats[slot, half, 0], stats[slot, half, 1]
@@ -323,42 +344,35 @@
                 stats[slot, half, 0] = ms
                 stats[slot, half, 1] = ls
 
-    def quarter(t, carry):
+    def stage(t, carry):
         @pl.when(t == 1)
         def _():
             for o in range(GROUPS):
                 spread(o, xpart, xs, xr, q).wait_recv()
-                spread(o, xpart, fs, fr, core).start()
-            for o in range(GROUPS):
-                spread(o, core, cs, cr, q).wait_recv()
-
-        @pl.when(t == 3)
-        def _():
-            for o in range(GROUPS):
-                spread(o, xcore, fs, fr, q).wait_recv()
-
-        holder = ((xx + t // 2) % 2) * 2 + (cc + t) % 2
-        own = jnp.where(t == 0, 1, 0).astype(jnp.int32)
+
+        column = (xx + t) % 2
+        own = 1 - t
 
         def one(n, inner):
-            k = holder * 2 + n % 2
+            k = (column * 2 + cc) * 2 + n % 2
+            kl = column * 2 + n % 2
             slot = (xx + 1 + n // 2) % 2
-            step(slot, k, own)
+            step(slot, k, kl, own)
 
             @pl.when(n < 2)
             def _():
-                acc_send(slot, 0, k, os0, (1 - xx) * 2).start()
-                acc_send(slot, 1, k, os1, (1 - xx) * 2 + 1).start()
+                acc_send(slot, 0, kl, os0, (1 - xx) * 2).start()
+                acc_send(slot, 1, kl, os1, (1 - xx) * 2 + 1).start()
 
             @pl.when(n >= 2)
             def _():
-                acc_send(slot, 1 - cc, k, os2, core).start()
+                acc_send(slot, 1 - cc, kl, os2, core).start()
 
             return inner
 
         return lax.fori_loop(0, 4, one, carry)
 
-    lax.fori_loop(0, 4, quarter, 0)
+    lax.fori_loop(0, 2, stage, 0)
 
     def stat_send(slot, half, n, to):
         return remote(stats.at[slot, half], rstat.at[q], ss.at[n], srs.at[q], (g, to))
@@ -372,21 +386,27 @@
 
     for other in (core, xpart, xcore):
         from_stat(other).wait_recv()
-    tops = [stats[xx, cc, 0]] + [rstat[other, 0] for other in (core, xpart, xcore)]
-    sums = [stats[xx, cc, 1]] + [rstat[other, 1] for other in (core, xpart, xcore)]
-    top = functools.reduce(jnp.maximum, tops)
-    factors = [jnp.exp2((m - top) * SCALE2) for m in tops]
-    total = sum(f * l for f, l in zip(factors, sums))
-    factors = [f / total for f in factors]
-
+    rstat[q] = stats[xx, cc]
+    rbuf[q] = accs[xx, cc]
+    factors = []
+    for parity in range(2):
+        pair = (xx * 2 + parity, (1 - xx) * 2 + parity)
+        tops = [rstat[other, 0] for other in pair]
+        top = jnp.maximum(tops[0], tops[1])
+        scaled = [jnp.exp2((m - top) * SCALE2) for m in tops]
+        total = scaled[0] * rstat[pair[0], 1] + scaled[1] * rstat[pair[1], 1]
+        factors.append([f / total for f in scaled])
+
+    for kl in range(4):
+        for other in (core, xpart, xcore):
+            remote(accs.at[0, 0, kl], rbuf.at[other, kl], os0.at[kl], ors.at[other, kl], (g, q)).wait_recv()
     for k in range(8):
-        for other in (core, xpart, xcore):
-            remote(accs.at[0, 0, k], rbuf.at[other, k], os0.at[k], ors.at[other, k], (g, q)).wait_recv()
-        terms = [accs[xx, cc, k]] + [rbuf[other, k] for other in (core, xpart, xcore)]
+        parity, kl = (k // 2) % 2, (k // 4) * 2 + k % 2
+        terms = [rbuf[xx * 2 + parity, kl], rbuf[(1 - xx) * 2 + parity, kl]]
         terms = [term.astype(jnp.float32).reshape(8, HALF, 128) for term in terms]
         for hh in range(8):
             h = k * 8 + hh
-            value = sum(f[:, h : h + 1] * term[hh] for f, term in zip(factors, terms))
+            value = sum(f[:, h : h + 1] * term[hh] for f, term in zip(factors[parity], terms))
             out_ref[:, h * 128 : (h + 1) * 128] = value.astype(jnp.bfloat16)
 
     for o in range(1, GROUPS):
@@ -403,9 +423,9 @@
 
     for o in range(GROUPS):
         spread(o, q, xs, xr, xpart).wait_send()
-        spread(o, q, cs, cr, core).wait_send()
-        spread(o, xpart, fs, fr, core).wait_send()
-    for k in range(8):
+    for n in range(8):
+        kv_swap(n // 4, n % 4).wait_send()
+    for k in range(4):
         acc_send(1 - xx, 0, k, os0, (1 - xx) * 2).wait_send()
         acc_send(1 - xx, 1, k, os1, (1 - xx) * 2 + 1).wait_send()
         acc_send(xx, 1 - cc, k, os2, core).wait_send()
@@ -431,14 +451,15 @@
             pltpu.VMEM((GROUPS, 2, TOK, 128), bf),
             pltpu.VMEM((2, 64, TOK, 128), bf),
             pltpu.VMEM((2, 4, TOK, 128), bf),
-            pltpu.VMEM((16, 2048, 256), bf),
-            pltpu.VMEM((2, 2, 8, ROWS, 128), bf),
-            pltpu.VMEM((QUARTERS, 8, ROWS, 128), bf),
+            pltpu.VMEM((8, 2, 2048, 256), bf),
+            pltpu.VMEM((2, 2, 4, ROWS, 128), bf),
+            pltpu.VMEM((QUARTERS, 4, ROWS, 128), bf),
             pltpu.VMEM((2, 2, 2, HALF, 128), jnp.float32),
             pltpu.VMEM((QUARTERS, 2, HALF, 128), jnp.float32),
         ]
-        + [dma((GROUPS,))] * 14
-        + [dma((16,)), dma((8,)), dma((8,)), dma((8,)), dma((QUARTERS, 8)), dma((3,)), dma((QUARTERS,))],
+        + [dma((GROUPS,))] * 10
+        + [dma((8,))] * 3
+        + [dma((4,)), dma((4,)), dma((4,)), dma((QUARTERS, 4)), dma((3,)), dma((QUARTERS,))],
         compiler_params=pltpu.CompilerParams(
             collective_id=0, has_side_effects=True, vmem_limit_bytes=56 * 1024 * 1024
         ),

time: 67.6 us -> 58.1 us (0.86)
  Pallas kernels: 64.2 us -> 54.7 us
    pallas_call x1, Pallas kernels: 64.2 us -> 54.7 us  [fused(): pl.pallas_call(fused_kernel, out_shape=jax.ShapeDtypeStruct((HALF, 8192),...]
where the time goes in v2:
time: 58.1 us; the launch traced here: 57.9 us
  Pallas kernels  54.7 us (94%)
  local copies, waits for them, and re-layouts  1.77 us (3%)
  matrix products  0.8 us (1%)
  between operations  0.67 us (1%)
    pallas_call x1, Pallas kernels, fused(): pl.pallas_call(fused_kernel, out_shape=jax.ShapeDtypeStruct((HALF, 8192),...  54.7 us
    unnamed x5, local copies, waits for them, and re-layouts  1.77 us

profile of v2, /device:TPU:29, one launch (start us, length us, event | category | flops | bytes accessed | tf_op | source)
XLA Modules:
  0.0 57.9 jit_solution(13778670776896751402)
XLA Ops:
  0.6 0.0 copy-start
  0.6 0.0 copy-start.1
  0.7 54.7 %shard_map.86 = bf16[24,8192]{1,0:T(8,128)(2,1)} custom-call(s32[16]{0:T(128)} %deal.1, s32[2]{0:T(128)} %lens.1, bf16[2,48,2048]{2,1,0:T(8,128)(2,1)} %q_ref.1, bf16[2,48,512]{2,1,0:T(8,128)(2,1)} %d_ref.1, bf16[2,2048,2048]{2,1,0:T(8,128)(2,1)} %kv_ref.1, s32[2,48,48]{2,1,0:T(8,128)} %anc_ref.1), custom_call_target="tpu_custom_call" | custom-call | flops 2000000000 | bytes 18000000 | tf_op jit(solution)/shard_map/pallas_call | solution.py:442
  55.3 0.0 copy-done
  55.3 0.0 copy-done.1
  55.4 0.8 %convolution_convert_fusion = bf16[2,8,512]{2,1,0:T(8,128)(2,1)} fusion(bf16[2,48,512]{2,1,0:T(8,128)(2,1)S(1)} %copy-done, s32[2,8]{1,0:T(2,128)S(1)} %copy-done.1), kind=kOutput, calls=%fused_computation | convolution fusion | flops 795392 | bytes 114752 | tf_op jit(solution)/shard_map/rit,rtc->ric/dot_general | solution.py:483
  56.1 1.8 %copy.10 = bf16[24,8192]{1,0:T(8,128)(2,1)} copy(bf16[24,8192]{1,0:T(8,128)(2,1)} %shard_map.86) | data formatting | bytes 786432
Async XLA Ops:
  0.6 54.7 %copy-start = (bf16[2,48,512]{2,1,0:T(8,128)(2,1)S(1)}, bf16[2,48,512]{2,1,0:T(8,128)(2,1)}, u32[]{:S(2)}) copy-start(bf16[2,48,512]{2,1,0:T(8,128)(2,1)} %d_ref.1) | copy-start | bytes 294916
  0.6 54.7 %copy-start.1 = (s32[2,8]{1,0:T(2,128)S(1)}, s32[2,8]{1,0:T(2,128)}, u32[]{:S(2)}) copy-start(s32[2,8]{1,0:T(2,128)} %param.13) | copy-start | bytes 196
